TPU v7x, 128 devices: a whole 4x4x4 slice. The times are simulated.
128 devices in a mesh: front: 8 (over z, x_lo), row: 8 (over x_hi, y), col: 2 (over core).
Axes of the slice: x: 4 (x_hi: 2, x_lo: 2; x = x_hi * 2 + x_lo), y: 4, z: 4, core: 2. Of those that a mesh axis runs over, the one named last changes fastest.
Arguments:
- front_matrix: float32 [8, 12, 1024, 3072], P('front', None, 'row', 'col')
- front_sizes: int32 [8], P('front'), may hold values from 8192 to 12288, as said below
- contrib: float32 [8, 4, 1024, 3072], P('front', None, 'row', 'col'), may hold values from -6 to 6
- dest_front: int32 [8, 4, 8], P('front', None, 'row'), may hold values from 0 to 7, as said below
- dest_local: int32 [8, 4, 8], P('front', None, 'row'), may hold values from 1 to 11, as said below
Outputs:
- factored: float32 [8, 12, 1024, 3072], P('front', None, 'row', 'col')
Inputs may be any that keep to these rules, and one draw needn't show every extreme that they name: `front_sizes`: multiples of 128; every draw has a front of order 12288 and one of order 8192. For each (g, r), the 4 entries dest_front[g, :, r] name distinct fronts. The block (g, k, r) lands on parent rows from (dest_local * 8 + r) * 128: at or after row 1024 and wholly below the parent's order; several blocks may land on the same rows; in every draw some block lands in the last round of blocks of the largest front.
All inputs are finite; a program needn't handle non-finite values.
Results may differ from a plain program's by a relative error of at most 0.0003.
Values sent between devices are 32-bit elements; how exact they have to be, the bound alone decides.
A program may use at most 128 MiB of HBM per device.

v0:
```python
import jax
import jax.numpy as jnp
from jax import lax
from jax.sharding import PartitionSpec as P

PW = 512
NPANEL = 2
W = 3072


def broadcast(value, axis, source):
    kept = jnp.where(lax.axis_index(axis) == source, value, 0).astype(value.dtype)
    return lax.psum(kept, axis)


def lower_inverse(pivot_block):
    symmetric = jnp.tril(pivot_block) + jnp.tril(pivot_block, -1).T
    factor = jnp.linalg.cholesky(symmetric)
    eye_block = jnp.eye(factor.shape[0], dtype=jnp.float32)
    inverse = jax.scipy.linalg.solve_triangular(factor, eye_block, lower=True)
    return (factor, inverse)


def on_device(front_matrix, front_sizes, contrib, dest_front, dest_local):
    front_count = lax.axis_size("front")
    row_count = lax.axis_size("row")
    row_here = lax.axis_index("row")
    col_here = lax.axis_index("col")
    local_blocks = front_matrix.shape[1]
    block_rows = front_matrix.shape[2]
    half_width = front_matrix.shape[3]
    half_rows = block_rows // 2
    cycle_rows = row_count * block_rows
    local_rows = local_blocks * block_rows
    window_blocks = W // cycle_rows
    block_ids = jnp.arange(local_blocks, dtype=jnp.int32)
    global_row = (
        block_ids[:, None] * cycle_rows
        + row_here * block_rows
        + jnp.arange(block_rows, dtype=jnp.int32)[None, :]
    ).reshape(local_rows)
    global_col = col_here * half_width + jnp.arange(half_width, dtype=jnp.int32)
    matrix = front_matrix[0].reshape(local_rows, half_width)
    matrix = jnp.where((global_row < front_sizes[0])[:, None], matrix, 0.0)
    targets = dest_front[0, :, 0]
    places = dest_local[0, :, 0]
    fronts_all = jnp.arange(front_count, dtype=jnp.int32)
    select = targets[None, :] == fronts_all[:, None]
    outgoing = jnp.einsum(
        "fk,kiw->fiw", select.astype(jnp.float32), contrib[0], precision=lax.Precision.HIGHEST
    )
    slot_place = jnp.where(
        jnp.any(select, axis=1), jnp.sum(jnp.where(select, places[None, :], 0), axis=1), -1
    )
    incoming, in_place = (
        lax.all_to_all(outgoing, "front", split_axis=0, concat_axis=0, tiled=True),
        lax.all_to_all(slot_place, "front", split_axis=0, concat_axis=0, tiled=True),
    )
    placing = (in_place[None, :] == block_ids[:, None]).astype(jnp.float32)
    placed_rows = jnp.einsum("ls,siw->liw", placing, incoming, precision=lax.Precision.HIGHEST)
    matrix = matrix + placed_rows.reshape(local_rows, half_width)
    for panel_index in range(NPANEL):
        col_start = panel_index * PW
        owned_columns = matrix[:, col_start : col_start + PW]
        columns = broadcast(owned_columns, "col", 0)
        first_block = col_start // block_rows
        pivot_block = first_block // row_count
        offset = first_block % row_count * block_rows
        col_blocks = columns.reshape(local_blocks, block_rows, PW)
        row_piece = lax.dynamic_slice_in_dim(
            col_blocks[pivot_block], col_here * half_rows, half_rows, 0
        )
        gathered = lax.all_gather(row_piece, ("row", "col"), axis=0, tiled=True)
        factor, inverse = lower_inverse(gathered[offset : offset + PW])
        solved = jnp.dot(columns, inverse.T, precision=lax.Precision.HIGHEST)
        solved = jnp.where((global_row < col_start)[:, None], 0.0, solved)
        global_first = (pivot_block * row_count + row_here) * block_rows
        in_pivot = (global_first >= col_start) & (global_first < col_start + PW)
        pivot_piece = lax.dynamic_slice_in_dim(
            factor, jnp.clip(global_first - col_start, 0, PW - block_rows), block_rows, 0
        )
        current = solved[pivot_block * block_rows : (pivot_block + 1) * block_rows]
        solved = solved.at[pivot_block * block_rows : (pivot_block + 1) * block_rows].set(
            jnp.where(in_pivot, pivot_piece, current)
        )
        solved_blocks = solved.reshape(local_blocks, block_rows, PW)
        row_piece = lax.dynamic_slice_in_dim(
            solved_blocks[:window_blocks], col_here * half_rows, half_rows, 1
        )
        window_factor = lax.all_gather(row_piece, ("row", "col"), axis=1, tiled=True).reshape(W, PW)
        mine_cols = lax.dynamic_slice_in_dim(window_factor, col_here * half_width, half_width, 0)
        update = jnp.dot(solved, mine_cols.T, precision=lax.Precision.HIGHEST)
        active = (global_row >= col_start + PW)[:, None] & (global_col >= col_start + PW)[None, :]
        matrix = matrix - jnp.where(active, update, 0.0)
        replaced = jnp.where(col_here == 0, solved, matrix[:, col_start : col_start + PW])
        matrix = matrix.at[:, col_start : col_start + PW].set(replaced)
    upper_part = (global_row < NPANEL * PW)[:, None] & (global_col >= NPANEL * PW)[None, :]
    matrix = jnp.where(upper_part, 0.0, matrix)
    return matrix.reshape(1, local_blocks, block_rows, half_width)


def solution(mesh):
    return jax.shard_map(
        on_device,
        mesh=mesh,
        in_specs=(
            P("front", None, "row", "col"),
            P("front"),
            P("front", None, "row", "col"),
            P("front", None, "row"),
            P("front", None, "row"),
        ),
        out_specs=P("front", None, "row", "col"),
        check_vma=False,
    )
```

profile of v0, /device:TPU:1, one launch (start us, length us, event | category | flops | bytes accessed | tf_op | source)
XLA Modules:
  0.0 793.3 jit_solution(2299873840947495213)
XLA Ops:
  8.9 6.8 all-to-all-start
  15.7 6.5 fusion.4
  22.2 6.3 copy.24
  28.6 5.1 all-to-all-start.1
  35.2 69.0 %all-to-all-done.1 = f32[8,128,1536]{2,1,0:T(8,128)} async-done(((f32[8,128,1536]{2,1,0:T(8,128)}), f32[8,128,1536]{2,1,0:T(8,128)}, u32[]{:S(2)}, u32[]{:S(2)}) %all-to-all-start.1) | async-done | bytes 6291488 | tf_op jit(solution)/shard_map/all_to_all | solution.py:56
  104.2 12.9 %fusion = f32[12,128,1536]{2,0,1:T(8,128)} fusion(f32[8,128,1536]{2,1,0:T(8,128)} %all-to-all-done.1, s32[8]{0:T(128)S(1)} %reduce.34), kind=kOutput, calls=%fused_computation.9 | convolution fusion | flops 226492512 | bytes 15728672 | tf_op jit(solution)/shard_map/ls,siw->liw/dot_general | solution.py:60
  117.1 13.8 %copy.26 = f32[12,128,1536]{2,1,0:T(8,128)} copy(f32[12,128,1536]{2,0,1:T(8,128)} %fusion) | data formatting | bytes 18874368 | tf_op jit(solution)/shard_map/ls,siw->liw/dot_general | solution.py:60
  130.9 11.0 %bitcast_add_fusion = f32[1536,1536]{1,0:T(8,128)} fusion(f32[12,128,1536]{2,1,0:T(8,128)} %copy.26, f32[1,12,128,1536]{3,2,1,0:T(8,128)} %param.16, pred[1536]{0:T(1024)(128)(4,1)S(1)} %get-tuple-element.120), kind=kLoop, calls=%fused_computation.4 | loop fusion | flops 4718592 | bytes 28313088 | tf_op jit(solution)/shard_map/add | solution.py:61
  141.9 3.9 slice_select_fusion.1
  145.9 30.6 %all-reduce.4.cloned.1.call-done = f32[1536,512]{1,0:T(8,128)} async-done(((f32[1536,512]{1,0:T(8,128)}), f32[1536,512]{1,0:T(8,128)}) %all-reduce.4.cloned.1.call-update) | async-done | bytes 3145744 | tf_op jit(solution)/shard_map/psum | solution.py:13
  176.5 1.0 slice.220
  178.5 49.5 %all-gather.5.cloned.1.call-done = f32[1024,512]{1,0:T(8,128)} async-done(((f32[64,512]{1,0:T(8,128)}), f32[1024,512]{1,0:T(8,128)}) %all-gather.5.cloned.1.call-update) | async-done | bytes 2097168 | tf_op jit(solution)/shard_map/all_gather | solution.py:73
  228.0 1.3 slice.221
  229.7 1.4 bitcast_add_fusion.4
  232.7 11.7 %cholesky.286 = f32[128,128]{1,0:T(8,128)S(1)} custom-call(f32[128,128]{1,0:T(8,128)S(1)} %cholesky.426), custom_call_target="Cholesky" | custom-call | tf_op jit(solution)/shard_map/jit(cholesky)/cholesky | solution.py:18
  244.4 9.8 %custom-call.27 = f32[1,128,128]{1,2,0:T(8,128)S(1)} custom-call(f32[1,128,128]{2,1,0:T(8,128)S(1)} %get-tuple-element.114), custom_call_target="InvertDiagBlocksLowerTriangular" | custom-call | tf_op jit(solution)/shard_map/jit(cholesky)/cholesky | solution.py:18
  254.3 1.2 constant_dynamic-update-slice_fusion.1
  255.6 1.3 convolution_subtract_fusion.7
  256.9 11.7 %cholesky.305 = f32[128,128]{1,0:T(8,128)S(1)} custom-call(f32[128,128]{1,0:T(8,128)S(1)} %cholesky.430), custom_call_target="Cholesky" | custom-call | tf_op jit(solution)/shard_map/jit(cholesky)/cholesky | solution.py:18
  268.6 10.0 %custom-call.28 = f32[1,128,128]{1,2,0:T(8,128)S(1)} custom-call(f32[1,128,128]{2,1,0:T(8,128)S(1)} %get-tuple-element.111), custom_call_target="InvertDiagBlocksLowerTriangular" | custom-call | tf_op jit(solution)/shard_map/jit(cholesky)/cholesky | solution.py:18
  278.9 1.3 convolution_subtract_fusion.9
  280.2 11.7 %cholesky.326 = f32[128,128]{1,0:T(8,128)S(1)} custom-call(f32[128,128]{1,0:T(8,128)S(1)} %cholesky.435), custom_call_target="Cholesky" | custom-call | tf_op jit(solution)/shard_map/jit(cholesky)/cholesky | solution.py:18
  292.7 9.8 %custom-call.29 = f32[1,128,128]{1,2,0:T(8,128)S(1)} custom-call(f32[1,128,128]{2,1,0:T(8,128)S(1)} %get-tuple-element.108), custom_call_target="InvertDiagBlocksLowerTriangular" | custom-call | tf_op jit(solution)/shard_map/jit(cholesky)/cholesky | solution.py:18
  302.7 1.2 convolution_subtract_fusion.11
  303.9 12.1 %cholesky.343 = f32[128,128]{1,0:T(8,128)S(1)} custom-call(f32[128,128]{1,0:T(8,128)S(1)} %convolution_subtract_fusion.11), custom_call_target="Cholesky" | custom-call | tf_op jit(solution)/shard_map/jit(cholesky)/cholesky | solution.py:18
  320.1 1.2 fusion.26
  321.3 8.4 %while.8 = (s32[]{:T(128)}, f32[512,512]{1,0:T(8,128)S(1)}, s32[4,2]{0,1:T(2,128)S(1)}, f32[4,128,128]{2,1,0:T(8,128)S(1)}, s32[]{:T(128)}) while((s32[]{:T(128)}, f32[512,512]{1,0:T(8,128)S(1)}, s32[4,2]{0,1:T(2,128)S(1)}, f32[4,128,128]{2,1,0:T(8,128)S(1)}, s32[]{:T(128)}) %tuple.74), condition=%wide.while_cond.4, body=%wide.while_body.4.sunk | while | flops 2 | bytes 131181 | solution.py:20
  322.0 1.4 bitcast_dynamic-update-slice_fusion.4
  324.1 1.4 bitcast_dynamic-update-slice_fusion.4
  326.2 1.4 bitcast_dynamic-update-slice_fusion.4
  328.3 1.4 bitcast_dynamic-update-slice_fusion.4
  329.8 39.3 %custom-call.30 = f32[4,128,128]{1,2,0:T(8,128)S(1)} custom-call(f32[4,128,128]{2,1,0:T(8,128)S(1)} %get-tuple-element.69), custom_call_target="InvertDiagBlocksLowerTriangular" | custom-call | tf_op jit(solution)/shard_map/jit(_solve_triangular)/triangular_solve | solution.py:20
  372.2 7.1 convolution_select_fusion.1
  379.3 1.0 fusion.46
  382.1 62.1 %all-gather.7.cloned.1.call-done = f32[3,1024,512]{2,1,0:T(8,128)} async-done(((f32[3,64,512]{2,1,0:T(8,128)}), f32[3,1024,512]{2,1,0:T(8,128)}) %all-gather.7.cloned.1.call-update) | async-done | bytes 6291472 | tf_op jit(solution)/shard_map/all_gather | solution.py:90
  444.2 19.2 %select_subtract_fusion.1 = f32[1536,1536]{1,0:T(8,128)S(1)} fusion(f32[1536,1536]{1,0:T(8,128)} %bitcast_add_fusion, f32[1536,512]{1,0:T(8,128)S(1)} %fusion.46, pred[1536]{0:T(1024)(128)(4,1)S(1)} %fusion.84, pred[1536]{0:T(1024)(128)(4,1)S(1)} %get-tuple-element.119, f32[3072,512]{1,0:T(8,128)} %bitcast.143, s32[]{:T(128)S(6)} %select_n.117), kind=kOutput, calls=%fused_computation.7 | convolution fusion | flops 14502592512 | bytes 25168900 | tf_op jit(solution)/shard_map/dot_general | solution.py:92
  463.4 1.5 fusion.2
  464.9 3.7 copy-done.2
  468.7 2.1 slice_select_fusion
  470.8 26.8 %all-reduce.6.cloned.1.call-done = f32[1536,512]{1,0:T(8,128)} async-done(((f32[1536,512]{1,0:T(8,128)}), f32[1536,512]{1,0:T(8,128)}) %all-reduce.6.cloned.1.call-update) | async-done | bytes 3145744 | tf_op jit(solution)/shard_map/psum | solution.py:13
  497.6 1.0 slice.226
  500.0 48.7 %all-gather.9.cloned.1.call-done = f32[1024,512]{1,0:T(8,128)} async-done(((f32[64,512]{1,0:T(8,128)}), f32[1024,512]{1,0:T(8,128)}) %all-gather.9.cloned.1.call-update) | async-done | bytes 2097168 | tf_op jit(solution)/shard_map/all_gather | solution.py:73
  548.7 1.4 slice_select_fusion.2
  550.4 1.4 bitcast_add_fusion.2
  552.4 11.7 %cholesky.358 = f32[128,128]{1,0:T(8,128)S(1)} custom-call(f32[128,128]{1,0:T(8,128)S(1)} %cholesky.439), custom_call_target="Cholesky" | custom-call | tf_op jit(solution)/shard_map/jit(cholesky)/cholesky | solution.py:18
  564.3 9.8 %custom-call.31 = f32[1,128,128]{1,2,0:T(8,128)S(1)} custom-call(f32[1,128,128]{2,1,0:T(8,128)S(1)} %get-tuple-element.104), custom_call_target="InvertDiagBlocksLowerTriangular" | custom-call | tf_op jit(solution)/shard_map/jit(cholesky)/cholesky | solution.py:18
  574.8 11.7 %cholesky.377 = f32[128,128]{1,0:T(8,128)S(1)} custom-call(f32[128,128]{1,0:T(8,128)S(1)} %cholesky.443), custom_call_target="Cholesky" | custom-call | tf_op jit(solution)/shard_map/jit(cholesky)/cholesky | solution.py:18
  587.8 10.2 %custom-call.32 = f32[1,128,128]{1,2,0:T(8,128)S(1)} custom-call(f32[1,128,128]{2,1,0:T(8,128)S(1)} %get-tuple-element.101), custom_call_target="InvertDiagBlocksLowerTriangular" | custom-call | tf_op jit(solution)/shard_map/jit(cholesky)/cholesky | solution.py:18
  598.7 11.7 %cholesky.398 = f32[128,128]{1,0:T(8,128)S(1)} custom-call(f32[128,128]{1,0:T(8,128)S(1)} %cholesky.448), custom_call_target="Cholesky" | custom-call | tf_op jit(solution)/shard_map/jit(cholesky)/cholesky | solution.py:18
  611.1 9.8 %custom-call.33 = f32[1,128,128]{1,2,0:T(8,128)S(1)} custom-call(f32[1,128,128]{2,1,0:T(8,128)S(1)} %get-tuple-element.98), custom_call_target="InvertDiagBlocksLowerTriangular" | custom-call | tf_op jit(solution)/shard_map/jit(cholesky)/cholesky | solution.py:18
  621.5 11.8 %cholesky.415 = f32[128,128]{1,0:T(8,128)S(1)} custom-call(f32[128,128]{1,0:T(8,128)S(1)} %convolution_subtract_fusion.10), custom_call_target="Cholesky" | custom-call | tf_op jit(solution)/shard_map/jit(cholesky)/cholesky | solution.py:18
  636.6 1.2 fusion.24
  637.9 8.1 %while.9 = (s32[]{:T(128)}, f32[512,512]{1,0:T(8,128)S(1)}, s32[4,2]{0,1:T(2,128)S(1)}, f32[4,128,128]{2,1,0:T(8,128)S(1)}, s32[]{:T(128)}) while((s32[]{:T(128)}, f32[512,512]{1,0:T(8,128)S(1)}, s32[4,2]{0,1:T(2,128)S(1)}, f32[4,128,128]{2,1,0:T(8,128)S(1)}, s32[]{:T(128)}) %tuple.92), condition=%wide.while_cond.4.clone, body=%wide.while_body.4.clone.sunk | while | flops 2 | bytes 131181 | solution.py:20
  638.6 1.3 bitcast_dynamic-update-slice_fusion.5
  640.6 1.3 bitcast_dynamic-update-slice_fusion.5
  642.6 1.3 bitcast_dynamic-update-slice_fusion.5
  644.6 1.3 bitcast_dynamic-update-slice_fusion.5
  646.0 39.3 %custom-call.34 = f32[4,128,128]{1,2,0:T(8,128)S(1)} custom-call(f32[4,128,128]{2,1,0:T(8,128)S(1)} %get-tuple-element.70), custom_call_target="InvertDiagBlocksLowerTriangular" | custom-call | tf_op jit(solution)/shard_map/jit(_solve_triangular)/triangular_solve | solution.py:20
  688.5 7.1 convolution_select_fusion
  695.6 1.0 fusion.44
  698.2 62.2 %all-gather.11.cloned.1.call-done = f32[3,1024,512]{2,1,0:T(8,128)} async-done(((f32[3,64,512]{2,1,0:T(8,128)}), f32[3,1024,512]{2,1,0:T(8,128)}) %all-gather.11.cloned.1.call-update) | async-done | bytes 6291472 | tf_op jit(solution)/shard_map/all_gather | solution.py:90
  760.5 19.3 %select_subtract_fusion = f32[1536,1536]{1,0:T(8,128)S(1)} fusion(f32[1536,1536]{1,0:T(8,128)} %copy-done.2, f32[1536,512]{1,0:T(8,128)S(1)} %fusion.44, pred[1536]{0:T(1024)(128)(4,1)S(1)} %fusion.85, pred[1536]{0:T(1024)(128)(4,1)S(1)} %get-tuple-element.117, f32[3072,512]{1,0:T(8,128)} %bitcast.144, s32[]{:T(128)S(6)} %select_n.117), kind=kOutput, calls=%fused_computation.6 | convolution fusion | flops 14502592512 | bytes 25168900 | tf_op jit(solution)/shard_map/dot_general | solution.py:92
  779.8 1.6 fusion.3
  781.4 4.7 and_select_fusion
  (116 shorter events, 31.1 us)
Async XLA Ops:
  6.5 9.2 %copy-start = (f32[1,4,128,1536]{3,2,1,0:T(8,128)S(1)}, f32[1,4,128,1536]{3,2,1,0:T(8,128)}, u32[]{:S(2)}) copy-start(f32[1,4,128,1536]{3,2,1,0:T(8,128)} %param.18) | copy-start | bytes 9437188
  8.9 19.6 %all-to-all-start = ((s32[8,1,1]{2,1,0:T(1,128)}), s32[8,1,1]{2,1,0:T(1,128)S(1)}, u32[]{:S(2)}, u32[]{:S(2)}) async-start(s32[8,1,1]{2,1,0:T(1,128)} %copy.22), calls=%async_computation | async-start | bytes 8192 | tf_op jit(solution)/shard_map/all_to_all | solution.py:57
  28.6 75.7 %all-to-all-start.1 = ((f32[8,128,1536]{2,1,0:T(8,128)}), f32[8,128,1536]{2,1,0:T(8,128)}, u32[]{:S(2)}, u32[]{:S(2)}) async-start(f32[8,128,1536]{2,1,0:T(8,128)} %copy.24), calls=%async_computation.1 | async-start | bytes 12582912 | tf_op jit(solution)/shard_map/all_to_all | solution.py:56
  33.7 142.8 %all-reduce.4.cloned.1.call-start = ((), (), s32[]{:S(2)}) async-start(), calls=%async_computation.2 | async-start | bytes 6291456 | tf_op jit(solution)/shard_map/psum | solution.py:13
  145.8 82.2 %all-gather.5.cloned.1.call-start = ((), (), s32[]{:S(2)}) async-start(), calls=%async_computation.3 | async-start | bytes 2228224 | tf_op jit(solution)/shard_map/all_gather | solution.py:73
  178.1 266.1 %all-gather.7.cloned.1.call-start = ((), (), s32[]{:S(2)}) async-start(), calls=%async_computation.4 | async-start | bytes 6684672 | tf_op jit(solution)/shard_map/all_gather | solution.py:90
  178.5 192.7 %copy-start.3 = (f32[512,512]{1,0:T(8,128)}, f32[512,512]{1,0:T(8,128)S(1)}, u32[]{:S(2)}) copy-start(f32[512,512]{1,0:T(8,128)S(1)} %fusion.27) | copy-start | bytes 3145732
  231.7 1.0 copy-start.5
  381.2 116.3 %all-reduce.6.cloned.1.call-start = ((), (), s32[]{:S(2)}) async-start(), calls=%async_computation.5 | async-start | bytes 6291456 | tf_op jit(solution)/shard_map/psum | solution.py:13
  464.9 3.7 copy-start.2
  470.8 77.9 %all-gather.9.cloned.1.call-start = ((), (), s32[]{:S(2)}) async-start(), calls=%async_computation.6 | async-start | bytes 2228224 | tf_op jit(solution)/shard_map/all_gather | solution.py:73
  499.2 261.2 %all-gather.11.cloned.1.call-start = ((), (), s32[]{:S(2)}) async-start(), calls=%async_computation.7 | async-start | bytes 6684672 | tf_op jit(solution)/shard_map/all_gather | solution.py:90
  586.5 98.8 %copy-start.4 = (f32[512,512]{1,0:T(8,128)S(1)}, f32[512,512]{1,0:T(8,128)}, u32[]{:S(2)}) copy-start(f32[512,512]{1,0:T(8,128)} %copy-done.3) | copy-start | bytes 3145732
  781.4 4.8 copy-start.1
Sparse Core Ops, SparseCore 0:
  145.9 30.4 all-reduce.3
  179.2 48.7 all-gather.4
  381.4 62.7 all-gather.6
  470.9 26.6 all-reduce.5
  499.9 48.7 all-gather.8
  697.6 62.7 all-gather.10
where the time goes:
time: 802 us; the launch traced here: 793 us
  waiting for transfers between devices  349 us (44%)
  other arithmetic  275 us (34%)
  matrix products  85.6 us (11%)
  local copies, waits for them, and re-layouts  50.2 us (6%)
  between operations  20.2 us (3%)
  starting transfers between devices  13.2 us (2%)
    another operation x29, other arithmetic, lower_inverse(): factor = jnp.linalg.cholesky(symmetric)  159 us
    all_gather x2, waiting for transfers between devices, on_device(): lax.all_gather(row_piece, ('row', 'col'), axis=1, tiled=True).reshape(W, PW)  124 us
    all_gather x2, waiting for transfers between devices, on_device(): gathered = lax.all_gather(row_piece, ('row', 'col'), axis=0, tiled=True)  98.2 us
    another operation x5, other arithmetic, lower_inverse(): inverse = jax.scipy.linalg.solve_triangular(factor, eye_block, lower=True)  81.1 us
    all_to_all x1, waiting for transfers between devices, on_device(): lax.all_to_all(outgoing, 'front', split_axis=0, concat_axis=0, tiled=True)  69 us
    psum x2, waiting for transfers between devices, broadcast(): return lax.psum(kept, axis)  57.3 us
    dot_general x2, matrix products, on_device(): update = jnp.dot(solved, mine_cols.T, precision=lax.Precision.HIGHEST)  38.5 us
    another operation x27, local copies, waits for them, and re-layouts, lower_inverse(): inverse = jax.scipy.linalg.solve_triangular(factor, eye_block, lower=True)  16.4 us
  transfers between devices with their start and end apart: 8, of which 7 were waited for; matrix products, arithmetic and copies ran while one was open for 2% of the time, Pallas kernels for 0%

commit v1 on v0

--- a/solution.py
+++ b/solution.py
@@ -1,11 +1,29 @@
+import functools
 import jax
 import jax.numpy as jnp
 from jax import lax
 from jax.sharding import PartitionSpec as P
+from jax.lax import all_to_all, axis_size
 
 PW = 512
 NPANEL = 2
 W = 3072
+
+
+def inputs_refer(tile_in, which_axis):
+    z = jnp.concatenate(
+        all_to_all(
+            jnp.stack(axis_size(which_axis) * [tile_in]),
+            axis_name=which_axis,
+            split_axis=0,
+            concat_axis=0,
+        ),
+        1,
+    )
+    return z
+
+
+supply_all_the_shelves = functools.partial(inputs_refer, which_axis=("row", "col"))
 
 
 def broadcast(value, axis, source):
@@ -87,7 +105,7 @@
         row_piece = lax.dynamic_slice_in_dim(
             solved_blocks[:window_blocks], col_here * half_rows, half_rows, 1
         )
-        window_factor = lax.all_gather(row_piece, ("row", "col"), axis=1, tiled=True).reshape(W, PW)
+        window_factor = supply_all_the_shelves(row_piece).reshape(W, PW)
         mine_cols = lax.dynamic_slice_in_dim(window_factor, col_here * half_width, half_width, 0)
         update = jnp.dot(solved, mine_cols.T, precision=lax.Precision.HIGHEST)
         active = (global_row >= col_start + PW)[:, None] & (global_col >= col_start + PW)[None, :]

time: 802 us -> 889 us (1.11)
  waiting for transfers between devices: 349 us -> 405 us
  local copies, waits for them, and re-layouts: 50.2 us -> 62.6 us
  starting transfers between devices: 13.2 us -> 22.5 us
    all_to_all x0 -> x2, waiting for transfers between devices: none -> 169 us  [inputs_refer(): all_to_all(jnp.stack(axis_size(which_axis) * [tile_in]), axis_name=which_...]
    all_gather x2 -> x0, waiting for transfers between devices: 124 us -> none  [on_device(): lax.all_gather(row_piece, ('row', 'col'), axis=1, tiled=True).reshape(W, PW)]
    psum x2, waiting for transfers between devices: 57.3 us -> 68.8 us  [broadcast(): return lax.psum(kept, axis)]
    all_to_all x0 -> x2, starting transfers between devices: none -> 9.44 us  [inputs_refer(): all_to_all(jnp.stack(axis_size(which_axis) * [tile_in]), axis_name=which_...]
where the time goes in v1:
time: 889 us; the launch traced here: 872 us
  waiting for transfers between devices  405 us (46%)
  other arithmetic  275 us (31%)
  matrix products  86.2 us (10%)
  local copies, waits for them, and re-layouts  62.6 us (7%)
  starting transfers between devices  22.5 us (3%)
  between operations  19.8 us (2%)
    all_to_all x2, waiting for transfers between devices, inputs_refer(): all_to_all(jnp.stack(axis_size(which_axis) * [tile_in]), axis_name=which_...  169 us
    another operation x29, other arithmetic, lower_inverse(): factor = jnp.linalg.cholesky(symmetric)  159 us
    all_gather x2, waiting for transfers between devices, on_device(): gathered = lax.all_gather(row_piece, ('row', 'col'), axis=0, tiled=True)  98.7 us
    another operation x5, other arithmetic, lower_inverse(): inverse = jax.scipy.linalg.solve_triangular(factor, eye_block, lower=True)  81.1 us
    all_to_all x1, waiting for transfers between devices, on_device(): lax.all_to_all(outgoing, 'front', split_axis=0, concat_axis=0, tiled=True)  69 us
    psum x2, waiting for transfers between devices, broadcast(): return lax.psum(kept, axis)  68.8 us
    dot_general x2, matrix products, on_device(): update = jnp.dot(solved, mine_cols.T, precision=lax.Precision.HIGHEST)  39.1 us
  transfers between devices with their start and end apart: 8, of which 7 were waited for; matrix products, arithmetic and copies ran while one was open for 2% of the time, Pallas kernels for 0%

profile of v1, /device:TPU:1, one launch (start us, length us, event | category | flops | bytes accessed | tf_op | source)
XLA Modules:
  0.0 871.5 jit_solution(10067522121072970045)
XLA Ops:
  8.9 6.8 all-to-all-start
  15.7 6.5 fusion.4
  22.2 6.3 copy.35
  28.6 5.1 all-to-all-start.1
  35.2 69.0 %all-to-all-done.1 = f32[8,128,1536]{2,1,0:T(8,128)} async-done(((f32[8,128,1536]{2,1,0:T(8,128)}), f32[8,128,1536]{2,1,0:T(8,128)}, u32[]{:S(2)}, u32[]{:S(2)}) %all-to-all-start.1) | async-done | bytes 6291488 | tf_op jit(solution)/shard_map/all_to_all | solution.py:74
  104.2 12.9 %fusion = f32[12,128,1536]{2,0,1:T(8,128)} fusion(f32[8,128,1536]{2,1,0:T(8,128)} %all-to-all-done.1, s32[8]{0:T(128)S(1)} %reduce.34), kind=kOutput, calls=%fused_computation.9 | convolution fusion | flops 226492512 | bytes 15728672 | tf_op jit(solution)/shard_map/ls,siw->liw/dot_general | solution.py:78
  117.1 13.8 %copy.37 = f32[12,128,1536]{2,1,0:T(8,128)} copy(f32[12,128,1536]{2,0,1:T(8,128)} %fusion) | data formatting | bytes 18874368 | tf_op jit(solution)/shard_map/ls,siw->liw/dot_general | solution.py:78
  130.9 11.0 %bitcast_add_fusion = f32[1536,1536]{1,0:T(8,128)} fusion(f32[12,128,1536]{2,1,0:T(8,128)} %copy.37, f32[1,12,128,1536]{3,2,1,0:T(8,128)} %param.16, pred[1536]{0:T(1024)(128)(4,1)S(1)} %get-tuple-element.120), kind=kLoop, calls=%fused_computation.4 | loop fusion | flops 4718592 | bytes 28313088 | tf_op jit(solution)/shard_map/add | solution.py:79
  141.9 3.9 slice_select_fusion.1
  146.1 30.4 %all-reduce.4.cloned.1.call-done = f32[1536,512]{1,0:T(8,128)} async-done(((f32[1536,512]{1,0:T(8,128)}), f32[1536,512]{1,0:T(8,128)}) %all-reduce.4.cloned.1.call-update) | async-done | bytes 3145744 | tf_op jit(solution)/shard_map/psum | solution.py:31
  178.3 49.7 %all-gather.3.cloned.1.call-done = f32[1024,512]{1,0:T(8,128)} async-done(((f32[64,512]{1,0:T(8,128)}), f32[1024,512]{1,0:T(8,128)}) %all-gather.3.cloned.1.call-update) | async-done | bytes 2097168 | tf_op jit(solution)/shard_map/all_gather | solution.py:91
  228.0 1.3 slice.221
  229.7 1.4 bitcast_add_fusion.4
  232.7 11.7 %cholesky.286 = f32[128,128]{1,0:T(8,128)S(1)} custom-call(f32[128,128]{1,0:T(8,128)S(1)} %cholesky.426), custom_call_target="Cholesky" | custom-call | tf_op jit(solution)/shard_map/jit(cholesky)/cholesky | solution.py:36
  244.4 9.8 %custom-call.27 = f32[1,128,128]{1,2,0:T(8,128)S(1)} custom-call(f32[1,128,128]{2,1,0:T(8,128)S(1)} %get-tuple-element.114), custom_call_target="InvertDiagBlocksLowerTriangular" | custom-call | tf_op jit(solution)/shard_map/jit(cholesky)/cholesky | solution.py:36
  254.3 1.2 constant_dynamic-update-slice_fusion.1
  255.6 1.3 convolution_subtract_fusion.7
  256.9 11.7 %cholesky.305 = f32[128,128]{1,0:T(8,128)S(1)} custom-call(f32[128,128]{1,0:T(8,128)S(1)} %cholesky.430), custom_call_target="Cholesky" | custom-call | tf_op jit(solution)/shard_map/jit(cholesky)/cholesky | solution.py:36
  268.6 10.0 %custom-call.28 = f32[1,128,128]{1,2,0:T(8,128)S(1)} custom-call(f32[1,128,128]{2,1,0:T(8,128)S(1)} %get-tuple-element.111), custom_call_target="InvertDiagBlocksLowerTriangular" | custom-call | tf_op jit(solution)/shard_map/jit(cholesky)/cholesky | solution.py:36
  278.9 1.3 convolution_subtract_fusion.9
  280.2 11.7 %cholesky.326 = f32[128,128]{1,0:T(8,128)S(1)} custom-call(f32[128,128]{1,0:T(8,128)S(1)} %cholesky.435), custom_call_target="Cholesky" | custom-call | tf_op jit(solution)/shard_map/jit(cholesky)/cholesky | solution.py:36
  292.6 9.8 %custom-call.29 = f32[1,128,128]{1,2,0:T(8,128)S(1)} custom-call(f32[1,128,128]{2,1,0:T(8,128)S(1)} %get-tuple-element.108), custom_call_target="InvertDiagBlocksLowerTriangular" | custom-call | tf_op jit(solution)/shard_map/jit(cholesky)/cholesky | solution.py:36
  303.9 12.1 %cholesky.343 = f32[128,128]{1,0:T(8,128)S(1)} custom-call(f32[128,128]{1,0:T(8,128)S(1)} %convolution_subtract_fusion.11), custom_call_target="Cholesky" | custom-call | tf_op jit(solution)/shard_map/jit(cholesky)/cholesky | solution.py:36
  321.3 8.4 while.8
  322.0 1.4 bitcast_dynamic-update-slice_fusion.4
  324.1 1.4 bitcast_dynamic-update-slice_fusion.4
  326.2 1.4 bitcast_dynamic-update-slice_fusion.4
  328.3 1.4 bitcast_dynamic-update-slice_fusion.4
  329.7 39.3 %custom-call.30 = f32[4,128,128]{1,2,0:T(8,128)S(1)} custom-call(f32[4,128,128]{2,1,0:T(8,128)S(1)} %get-tuple-element.69), custom_call_target="InvertDiagBlocksLowerTriangular" | custom-call | tf_op jit(solution)/shard_map/jit(_solve_triangular)/triangular_solve | solution.py:38
  372.2 7.1 convolution_select_fusion.1
  380.5 3.5 stack.4
  384.0 4.6 all-to-all-start.2
  389.4 84.3 %all-to-all-done.2 = f32[16,3,64,512]{3,2,1,0:T(8,128)} async-done(((f32[16,3,64,512]{3,2,1,0:T(8,128)}), f32[16,3,64,512]{3,2,1,0:T(8,128)}, u32[]{:S(2)}, u32[]{:S(2)}) %all-to-all-start.2) | async-done | bytes 6291488 | tf_op jit(solution)/shard_map/all_to_all | solution.py:15
  473.7 3.5 copy.41
  477.2 19.2 %select_subtract_fusion.1 = f32[1536,1536]{1,0:T(8,128)S(1)} fusion(f32[1536,1536]{1,0:T(8,128)} %bitcast_add_fusion, f32[1536,512]{1,0:T(8,128)S(1)} %fusion.46, pred[1536]{0:T(1024)(128)(4,1)S(1)} %fusion.84, pred[1536]{0:T(1024)(128)(4,1)S(1)} %get-tuple-element.119, f32[3072,512]{1,0:T(8,128)S(1)} %bitcast.145, s32[]{:T(128)S(6)} %select_n.117), kind=kOutput, calls=%fused_computation.7 | convolution fusion | flops 14502592512 | bytes 25169924 | tf_op jit(solution)/shard_map/dot_general | solution.py:110
  496.5 1.5 fusion.2
  498.0 3.7 copy-done.2
  501.7 2.1 slice_select_fusion
  504.1 38.3 %all-reduce.6.cloned.1.call-done = f32[1536,512]{1,0:T(8,128)} async-done(((f32[1536,512]{1,0:T(8,128)}), f32[1536,512]{1,0:T(8,128)}) %all-reduce.6.cloned.1.call-update) | async-done | bytes 3145744 | tf_op jit(solution)/shard_map/psum | solution.py:31
  544.6 49.0 %all-gather.5.cloned.1.call-done = f32[1024,512]{1,0:T(8,128)} async-done(((f32[64,512]{1,0:T(8,128)}), f32[1024,512]{1,0:T(8,128)}) %all-gather.5.cloned.1.call-update) | async-done | bytes 2097168 | tf_op jit(solution)/shard_map/all_gather | solution.py:91
  593.5 1.4 slice_select_fusion.2
  595.2 1.4 bitcast_add_fusion.2
  597.2 11.7 %cholesky.358 = f32[128,128]{1,0:T(8,128)S(1)} custom-call(f32[128,128]{1,0:T(8,128)S(1)} %cholesky.439), custom_call_target="Cholesky" | custom-call | tf_op jit(solution)/shard_map/jit(cholesky)/cholesky | solution.py:36
  609.1 9.8 %custom-call.31 = f32[1,128,128]{1,2,0:T(8,128)S(1)} custom-call(f32[1,128,128]{2,1,0:T(8,128)S(1)} %get-tuple-element.104), custom_call_target="InvertDiagBlocksLowerTriangular" | custom-call | tf_op jit(solution)/shard_map/jit(cholesky)/cholesky | solution.py:36
  619.6 11.7 %cholesky.377 = f32[128,128]{1,0:T(8,128)S(1)} custom-call(f32[128,128]{1,0:T(8,128)S(1)} %cholesky.443), custom_call_target="Cholesky" | custom-call | tf_op jit(solution)/shard_map/jit(cholesky)/cholesky | solution.py:36
  633.1 9.8 %custom-call.32 = f32[1,128,128]{1,2,0:T(8,128)S(1)} custom-call(f32[1,128,128]{2,1,0:T(8,128)S(1)} %get-tuple-element.101), custom_call_target="InvertDiagBlocksLowerTriangular" | custom-call | tf_op jit(solution)/shard_map/jit(cholesky)/cholesky | solution.py:36
  643.6 11.7 %cholesky.398 = f32[128,128]{1,0:T(8,128)S(1)} custom-call(f32[128,128]{1,0:T(8,128)S(1)} %cholesky.448), custom_call_target="Cholesky" | custom-call | tf_op jit(solution)/shard_map/jit(cholesky)/cholesky | solution.py:36
  656.0 9.8 %custom-call.33 = f32[1,128,128]{1,2,0:T(8,128)S(1)} custom-call(f32[1,128,128]{2,1,0:T(8,128)S(1)} %get-tuple-element.98), custom_call_target="InvertDiagBlocksLowerTriangular" | custom-call | tf_op jit(solution)/shard_map/jit(cholesky)/cholesky | solution.py:36
  666.4 11.9 %cholesky.415 = f32[128,128]{1,0:T(8,128)S(1)} custom-call(f32[128,128]{1,0:T(8,128)S(1)} %convolution_subtract_fusion.10), custom_call_target="Cholesky" | custom-call | tf_op jit(solution)/shard_map/jit(cholesky)/cholesky | solution.py:36
  681.5 1.2 fusion.24
  682.7 8.1 while.9
  683.4 1.3 bitcast_dynamic-update-slice_fusion.5
  685.4 1.3 bitcast_dynamic-update-slice_fusion.5
  687.5 1.3 bitcast_dynamic-update-slice_fusion.5
  689.5 1.3 bitcast_dynamic-update-slice_fusion.5
  690.9 39.3 %custom-call.34 = f32[4,128,128]{1,2,0:T(8,128)S(1)} custom-call(f32[4,128,128]{2,1,0:T(8,128)S(1)} %get-tuple-element.70), custom_call_target="InvertDiagBlocksLowerTriangular" | custom-call | tf_op jit(solution)/shard_map/jit(_solve_triangular)/triangular_solve | solution.py:38
  733.3 7.1 convolution_select_fusion
  741.6 3.5 stack.5
  745.0 4.8 all-to-all-start.3
  750.5 84.5 %all-to-all-done.3 = f32[16,3,64,512]{3,2,1,0:T(8,128)} async-done(((f32[16,3,64,512]{3,2,1,0:T(8,128)}), f32[16,3,64,512]{3,2,1,0:T(8,128)}, u32[]{:S(2)}, u32[]{:S(2)}) %all-to-all-start.3) | async-done | bytes 6291488 | tf_op jit(solution)/shard_map/all_to_all | solution.py:15
  835.0 3.5 copy.45
  838.5 19.9 %select_subtract_fusion = f32[1536,1536]{1,0:T(8,128)S(1)} fusion(f32[1536,1536]{1,0:T(8,128)} %copy-done.2, f32[1536,512]{1,0:T(8,128)S(1)} %fusion.44, pred[1536]{0:T(1024)(128)(4,1)S(1)} %fusion.85, pred[1536]{0:T(1024)(128)(4,1)S(1)} %get-tuple-element.117, f32[3072,512]{1,0:T(8,128)S(1)} %bitcast.146, s32[]{:T(128)S(6)} %select_n.117), kind=kOutput, calls=%fused_computation.6 | convolution fusion | flops 14502592512 | bytes 25169924 | tf_op jit(solution)/shard_map/dot_general | solution.py:110
  858.4 1.6 fusion.3
  860.0 4.7 and_select_fusion
  (118 shorter events, 36.3 us)
Async XLA Ops:
  6.5 9.2 %copy-start = (f32[1,4,128,1536]{3,2,1,0:T(8,128)S(1)}, f32[1,4,128,1536]{3,2,1,0:T(8,128)}, u32[]{:S(2)}) copy-start(f32[1,4,128,1536]{3,2,1,0:T(8,128)} %param.18) | copy-start | bytes 9437188
  8.9 19.6 %all-to-all-start = ((s32[8,1,1]{2,1,0:T(1,128)}), s32[8,1,1]{2,1,0:T(1,128)S(1)}, u32[]{:S(2)}, u32[]{:S(2)}) async-start(s32[8,1,1]{2,1,0:T(1,128)} %copy.33), calls=%async_computation | async-start | bytes 8192 | tf_op jit(solution)/shard_map/all_to_all | solution.py:75
  28.6 75.7 %all-to-all-start.1 = ((f32[8,128,1536]{2,1,0:T(8,128)}), f32[8,128,1536]{2,1,0:T(8,128)}, u32[]{:S(2)}, u32[]{:S(2)}) async-start(f32[8,128,1536]{2,1,0:T(8,128)} %copy.35), calls=%async_computation.1 | async-start | bytes 12582912 | tf_op jit(solution)/shard_map/all_to_all | solution.py:74
  33.7 142.8 %all-reduce.4.cloned.1.call-start = ((), (), s32[]{:S(2)}) async-start(), calls=%async_computation.4 | async-start | bytes 6291456 | tf_op jit(solution)/shard_map/psum | solution.py:31
  145.8 82.2 %all-gather.3.cloned.1.call-start = ((), (), s32[]{:S(2)}) async-start(), calls=%async_computation.5 | async-start | bytes 2228224 | tf_op jit(solution)/shard_map/all_gather | solution.py:91
  178.3 192.9 %copy-start.3 = (f32[512,512]{1,0:T(8,128)}, f32[512,512]{1,0:T(8,128)S(1)}, u32[]{:S(2)}) copy-start(f32[512,512]{1,0:T(8,128)S(1)} %fusion.27) | copy-start | bytes 3145732
  231.7 1.0 copy-start.5
  384.0 89.8 %all-to-all-start.2 = ((f32[16,3,64,512]{3,2,1,0:T(8,128)}), f32[16,3,64,512]{3,2,1,0:T(8,128)}, u32[]{:S(2)}, u32[]{:S(2)}) async-start(f32[16,3,64,512]{3,2,1,0:T(8,128)} %stack.4), calls=%async_computation.2 | async-start | bytes 12582912 | tf_op jit(solution)/shard_map/all_to_all | solution.py:15
  388.6 153.8 %all-reduce.6.cloned.1.call-start = ((), (), s32[]{:S(2)}) async-start(), calls=%async_computation.6 | async-start | bytes 6291456 | tf_op jit(solution)/shard_map/psum | solution.py:31
  498.0 3.7 copy-start.2
  503.8 89.7 %all-gather.5.cloned.1.call-start = ((), (), s32[]{:S(2)}) async-start(), calls=%async_computation.7 | async-start | bytes 2228224 | tf_op jit(solution)/shard_map/all_gather | solution.py:91
  631.3 98.8 %copy-start.4 = (f32[512,512]{1,0:T(8,128)S(1)}, f32[512,512]{1,0:T(8,128)}, u32[]{:S(2)}) copy-start(f32[512,512]{1,0:T(8,128)} %copy-done.3) | copy-start | bytes 3145732
  745.0 90.0 %all-to-all-start.3 = ((f32[16,3,64,512]{3,2,1,0:T(8,128)}), f32[16,3,64,512]{3,2,1,0:T(8,128)}, u32[]{:S(2)}, u32[]{:S(2)}) async-start(f32[16,3,64,512]{3,2,1,0:T(8,128)} %stack.5), calls=%async_computation.3 | async-start | bytes 12582912 | tf_op jit(solution)/shard_map/all_to_all | solution.py:15
  860.0 4.8 copy-start.1
Sparse Core Ops, SparseCore 0:
  145.9 30.4 all-reduce.3
  179.2 48.7 all-gather.2
  503.9 38.4 all-reduce.5
  544.7 48.7 all-gather.4
